TPU v7x, 512 devices: a whole 4x8x8 slice. The times are simulated.
512 devices in a mesh: dom: 128 (over z, y, core), sub: 4 (over x).
Axes of the slice: x: 4, y: 8, z: 8, core: 2. Of those that a mesh axis runs over, the one named last changes fastest.
Arguments:
- rhs: float32 [64, 8, 65536], P(None, None, ('dom', 'sub')), may hold values from -6 to 6
- guess: float32 [64, 8, 65536], P(None, None, ('dom', 'sub')), may hold values from -4 to 4
- diag_blocks: bfloat16 [2, 64, 64], replicated
- face_blocks: bfloat16 [6, 2, 64, 64], replicated, may hold values from -0.3125 to 0.3125
- smoother: bfloat16 [2, 64, 64], replicated
- coarse_inverse: bfloat16 [64, 64], replicated
- elem_type: int32 [65536], P(('dom', 'sub')), may hold values from 0 to 1
- face_type: int32 [6, 65536], P(None, ('dom', 'sub')), may hold values from 0 to 1
- neighbours: int32 [6, 65536], P(None, ('dom', 'sub')), may hold values from 0 to 239, as said below
- send_near: int32 [2, 16384], P(None, ('dom', 'sub')), may hold values from 0 to 127
- send_far: int32 [2, 4096], P(None, ('dom', 'sub')), may hold values from 0 to 127
- sub_send: int32 [4096], P(('dom', 'sub')), may hold values from 0 to 127
- partner: int32 [65536], P(('dom', 'sub')), may hold values from 0 to 143, as said below
- pair_send: int32 [8192], P(('dom', 'sub')), may hold values from 0 to 127, as said below
Outputs:
- solution: float32 [64, 8, 65536], P(None, None, ('dom', 'sub'))
- residual: float32 [64, 8, 65536], P(None, None, ('dom', 'sub'))
Inputs may be any that keep to these rules, and one draw needn't show every extreme that they name: `neighbours`: values below 128 are the device's own elements; the rest index its 112 received rows in the order of the first step. On each device the partner relation is mutual: local values pair two distinct local elements with each other; each value 128 + q for q below 16 appears exactly once, and the element holding it is entry q of the device's pair_send. `pair_send`: on each device the 16 entries are distinct; slot q pairs with slot q of the device whose sub index differs in the lowest bit.
All inputs are finite; a program needn't handle non-finite values.
Results may differ from a plain program's by a relative error of at most 0.012.
Values may be sent and summed in bfloat16 or wider, within the bound.
No kernel may reach another device: no remote copies, remote signals or barrier semaphores. Data moves between devices by JAX's collectives and lax.ppermute only.
A program may use at most 64 MiB of HBM per device.

v0:
```python
import jax
import jax.numpy as jnp
from jax import lax
from jax.sharding import PartitionSpec as P

SWEEPS = 2


def from_behind(array, axis, by):
    peers = lax.axis_size(axis)
    pairs = [(i, i + by) for i in range(peers) if 0 <= i + by < peers]
    return lax.ppermute(array, axis, pairs)


def partner_2(block, axis, stride):
    count = lax.axis_size(axis)
    route = []
    for low in range(count):
        high = low | 1 << stride
        if high != low and high < count:
            route += [(low, high), (high, low)]
    return lax.ppermute(block, axis, route)


def stack_apply(blocks, field_b, kinds):
    variants = blocks.shape[0]
    node_rows, rhs_width, elements = field_b.shape
    blank = jnp.zeros_like(field_b)
    pieces = [
        jnp.where(kinds[None, None, :] == variant, field_b, blank) for variant in range(variants)
    ]
    operand = jnp.concatenate(pieces, axis=0).reshape(variants * node_rows, rhs_width * elements)
    wide_blocks = jnp.concatenate([blocks[variant] for variant in range(variants)], axis=1)
    product = jnp.dot(wide_blocks, operand, preferred_element_type=jnp.float32)
    return product.reshape(node_rows, rhs_width, elements)


def body(
    rhs,
    guess,
    diag_blocks,
    face_blocks,
    smoother,
    coarse_inverse,
    elem_type,
    face_type,
    neighbours,
    send_near,
    send_far,
    sub_send,
    partner,
    pair_send,
):

    def apply_local(field_b):
        up_near = jnp.take(field_b, send_near[1], axis=2)
        down_near = jnp.take(field_b, send_near[0], axis=2)
        up_far = jnp.take(field_b, send_far[1], axis=2)
        down_far = jnp.take(field_b, send_far[0], axis=2)
        from_below = from_behind(up_near, "dom", 1)
        from_above = from_behind(down_near, "dom", -1)
        far_below = from_behind(up_far, "dom", 2)
        far_above = from_behind(down_far, "dom", -2)
        side_rows = lax.all_gather(jnp.take(field_b, sub_send, axis=2), "sub", axis=2, tiled=True)
        extended = jnp.concatenate(
            [field_b, from_below, from_above, far_below, far_above, side_rows], axis=2
        )
        total = stack_apply(diag_blocks, field_b, elem_type)
        for face_index in range(6):
            beside = jnp.take(extended, neighbours[face_index], axis=2)
            total = total + stack_apply(face_blocks[face_index], beside, face_type[face_index])
        return total

    iterate = guess
    for rounds in range(SWEEPS):
        sweep_res = rhs - apply_local(iterate.astype(jnp.bfloat16))
        iterate = iterate + stack_apply(smoother, sweep_res.astype(jnp.bfloat16), elem_type)
    residual = rhs - apply_local(iterate.astype(jnp.bfloat16))
    outgoing = jnp.take(residual, pair_send, axis=2)
    incoming = partner_2(outgoing.astype(jnp.bfloat16), "sub", 0).astype(outgoing.dtype)
    joined = jnp.concatenate([residual, incoming], axis=2)
    coarse = residual + jnp.take(joined, partner, axis=2)
    node_rows, rhs_width, elements = coarse.shape
    coarse_b = coarse.astype(jnp.bfloat16).reshape(node_rows, rhs_width * elements)
    update = jnp.dot(coarse_inverse, coarse_b, preferred_element_type=jnp.float32)
    solution = iterate + update.reshape(node_rows, rhs_width, elements)
    return (solution, residual)


def solution(mesh):
    in_specs = (
        P(None, None, ("dom", "sub")),
        P(None, None, ("dom", "sub")),
        P(),
        P(),
        P(),
        P(),
        P(("dom", "sub")),
        P(None, ("dom", "sub")),
        P(None, ("dom", "sub")),
        P(None, ("dom", "sub")),
        P(None, ("dom", "sub")),
        P(("dom", "sub")),
        P(("dom", "sub")),
        P(("dom", "sub")),
    )
    out_specs = (P(None, None, ("dom", "sub")), P(None, None, ("dom", "sub")))
    return jax.shard_map(body, mesh=mesh, in_specs=in_specs, out_specs=out_specs, check_vma=False)
```

profile of v0, /device:TPU:256, one launch (start us, length us, event | category | flops | bytes accessed | tf_op | source)
XLA Modules:
  0.0 147.1 jit_solution(16618105193743809623)
XLA Ops:
  0.7 0.7 broadcast_compare_fusion
  1.3 1.0 broadcast_select_fusion.27
  2.6 0.6 gather_fusion.2
  3.3 1.9 %collective-permute-start = (bf16[64,8,32]{2,0,1:T(8,128)(2,1)S(1)}, bf16[64,8,32]{2,0,1:T(8,128)(2,1)S(1)}, u32[]{:S(2)}, u32[]{:S(2)}) collective-permute-start(bf16[64,8,32]{2,0,1:T(8,128)(2,1)S(1)} %select_bitcast_fusion.5), channel_id=1, source_target_pairs={{0,4},{4,8},{8,12},{12,16},{16,20},{20,24},{24,28},{28,32},{32,36}... | collective-permute-start | bytes 98312 | tf_op jit(solution)/shard_map/ppermute | solution.py:12
  5.3 0.6 gather_fusion.3
  6.1 7.0 %collective-permute-start.1 = (bf16[64,8,32]{2,0,1:T(8,128)(2,1)S(1)}, bf16[64,8,32]{2,0,1:T(8,128)(2,1)S(1)}, u32[]{:S(2)}, u32[]{:S(2)}) collective-permute-start(bf16[64,8,32]{2,0,1:T(8,128)(2,1)S(1)} %select_bitcast_fusion.4), channel_id=1, source_target_pairs={{4,0},{8,4},{12,8},{16,12},{20,16},{24,20},{28,24},{32,28},{36,32}... | collective-permute-start | bytes 98312 | tf_op jit(solution)/shard_map/ppermute | solution.py:12
  13.7 1.9 %collective-permute-start.2 = (bf16[64,8,8]{0,1,2:T(8,128)(2,1)S(1)}, bf16[64,8,8]{0,1,2:T(8,128)(2,1)S(1)}, u32[]{:S(2)}, u32[]{:S(2)}) collective-permute-start(bf16[64,8,8]{0,1,2:T(8,128)(2,1)S(1)} %select_bitcast_fusion.14), channel_id=1, source_target_pairs={{0,8},{4,12},{8,16},{12,20},{16,24},{20,28},{24,32},{28,36},{32,40... | collective-permute-start | bytes 24584 | tf_op jit(solution)/shard_map/ppermute | solution.py:12
  16.3 7.2 %collective-permute-start.3 = (bf16[64,8,8]{0,1,2:T(8,128)(2,1)S(1)}, bf16[64,8,8]{0,1,2:T(8,128)(2,1)S(1)}, u32[]{:S(2)}, u32[]{:S(2)}) collective-permute-start(bf16[64,8,8]{0,1,2:T(8,128)(2,1)S(1)} %select_bitcast_fusion.13), channel_id=1, source_target_pairs={{8,0},{12,4},{16,8},{20,12},{24,16},{28,20},{32,24},{36,28},{40,32... | collective-permute-start | bytes 24584 | tf_op jit(solution)/shard_map/ppermute | solution.py:12
  25.6 12.2 %all_gather.9 = bf16[64,8,32]{0,1,2:T(8,128)(2,1)S(1)} all-gather(bf16[64,8,8]{0,1,2:T(8,128)(2,1)S(1)} %select_bitcast_fusion.12), channel_id=1, replica_groups=mesh['dom'=128,'sub'=4] {'sub'}, dimensions={2}, use_global_device_ids=true | all-gather | bytes 40960 | tf_op jit(solution)/shard_map/all_gather | solution.py:64
  38.8 0.7 gather_fusion.7
  40.0 0.7 gather_fusion.8
  41.1 0.7 gather_fusion.9
  42.2 0.7 gather_fusion.10
  43.4 0.7 gather_fusion.11
  44.5 0.7 gather_fusion.12
  47.0 0.7 copy-done.1
  48.2 0.7 copy-done.2
  49.4 0.6 gather_fusion.13
  50.0 0.6 gather_fusion.14
  52.9 1.9 %collective-permute-start.4 = (bf16[64,8,32]{2,0,1:T(8,128)(2,1)S(1)}, bf16[64,8,32]{2,0,1:T(8,128)(2,1)S(1)}, u32[]{:S(2)}, u32[]{:S(2)}) collective-permute-start(bf16[64,8,32]{2,0,1:T(8,128)(2,1)S(1)} %select_bitcast_fusion.3), channel_id=1, source_target_pairs={{0,4},{4,8},{8,12},{12,16},{16,20},{20,24},{24,28},{28,32},{32,36}... | collective-permute-start | bytes 98312 | tf_op jit(solution)/shard_map/ppermute | solution.py:12
  55.0 7.0 %collective-permute-start.5 = (bf16[64,8,32]{2,0,1:T(8,128)(2,1)S(1)}, bf16[64,8,32]{2,0,1:T(8,128)(2,1)S(1)}, u32[]{:S(2)}, u32[]{:S(2)}) collective-permute-start(bf16[64,8,32]{2,0,1:T(8,128)(2,1)S(1)} %select_bitcast_fusion.2), channel_id=1, source_target_pairs={{4,0},{8,4},{12,8},{16,12},{20,16},{24,20},{28,24},{32,28},{36,32}... | collective-permute-start | bytes 98312 | tf_op jit(solution)/shard_map/ppermute | solution.py:12
  62.1 1.9 %collective-permute-start.6 = (bf16[64,8,8]{0,1,2:T(8,128)(2,1)S(1)}, bf16[64,8,8]{0,1,2:T(8,128)(2,1)S(1)}, u32[]{:S(2)}, u32[]{:S(2)}) collective-permute-start(bf16[64,8,8]{0,1,2:T(8,128)(2,1)S(1)} %select_bitcast_fusion.11), channel_id=1, source_target_pairs={{0,8},{4,12},{8,16},{12,20},{16,24},{20,28},{24,32},{28,36},{32,40... | collective-permute-start | bytes 24584 | tf_op jit(solution)/shard_map/ppermute | solution.py:12
  64.1 7.2 %collective-permute-start.7 = (bf16[64,8,8]{0,1,2:T(8,128)(2,1)S(1)}, bf16[64,8,8]{0,1,2:T(8,128)(2,1)S(1)}, u32[]{:S(2)}, u32[]{:S(2)}) collective-permute-start(bf16[64,8,8]{0,1,2:T(8,128)(2,1)S(1)} %select_bitcast_fusion.10), channel_id=1, source_target_pairs={{8,0},{12,4},{16,8},{20,12},{24,16},{28,20},{32,24},{36,28},{40,32... | collective-permute-start | bytes 24584 | tf_op jit(solution)/shard_map/ppermute | solution.py:12
  71.4 12.0 %all_gather.10 = bf16[64,8,32]{0,1,2:T(8,128)(2,1)S(1)} all-gather(bf16[64,8,8]{0,1,2:T(8,128)(2,1)S(1)} %select_bitcast_fusion.9), channel_id=1, replica_groups=mesh['dom'=128,'sub'=4] {'sub'}, dimensions={2}, use_global_device_ids=true | all-gather | bytes 40960 | tf_op jit(solution)/shard_map/all_gather | solution.py:64
  84.5 0.7 gather_fusion.18
  85.2 0.7 gather_fusion.19
  85.9 0.7 gather_fusion.20
  86.5 0.7 gather_fusion.21
  87.2 0.7 gather_fusion.22
  87.9 0.7 gather_fusion.23
  93.6 0.6 gather_fusion.24
  94.2 0.6 gather_fusion.25
  97.1 1.9 %collective-permute-start.8 = (bf16[64,8,32]{2,0,1:T(8,128)(2,1)S(1)}, bf16[64,8,32]{2,0,1:T(8,128)(2,1)S(1)}, u32[]{:S(2)}, u32[]{:S(2)}) collective-permute-start(bf16[64,8,32]{2,0,1:T(8,128)(2,1)S(1)} %select_bitcast_fusion.1), channel_id=1, source_target_pairs={{0,4},{4,8},{8,12},{12,16},{16,20},{20,24},{24,28},{28,32},{32,36}... | collective-permute-start | bytes 98312 | tf_op jit(solution)/shard_map/ppermute | solution.py:12
  99.2 7.0 %collective-permute-start.9 = (bf16[64,8,32]{2,0,1:T(8,128)(2,1)S(1)}, bf16[64,8,32]{2,0,1:T(8,128)(2,1)S(1)}, u32[]{:S(2)}, u32[]{:S(2)}) collective-permute-start(bf16[64,8,32]{2,0,1:T(8,128)(2,1)S(1)} %select_bitcast_fusion), channel_id=1, source_target_pairs={{4,0},{8,4},{12,8},{16,12},{20,16},{24,20},{28,24},{32,28},{36,32}... | collective-permute-start | bytes 98312 | tf_op jit(solution)/shard_map/ppermute | solution.py:12
  106.3 1.9 %collective-permute-start.10 = (bf16[64,8,8]{0,1,2:T(8,128)(2,1)S(1)}, bf16[64,8,8]{0,1,2:T(8,128)(2,1)S(1)}, u32[]{:S(2)}, u32[]{:S(2)}) collective-permute-start(bf16[64,8,8]{0,1,2:T(8,128)(2,1)S(1)} %select_bitcast_fusion.8), channel_id=1, source_target_pairs={{0,8},{4,12},{8,16},{12,20},{16,24},{20,28},{24,32},{28,36},{32,40... | collective-permute-start | bytes 24584 | tf_op jit(solution)/shard_map/ppermute | solution.py:12
  108.3 7.2 %collective-permute-start.11 = (bf16[64,8,8]{0,1,2:T(8,128)(2,1)S(1)}, bf16[64,8,8]{0,1,2:T(8,128)(2,1)S(1)}, u32[]{:S(2)}, u32[]{:S(2)}) collective-permute-start(bf16[64,8,8]{0,1,2:T(8,128)(2,1)S(1)} %select_bitcast_fusion.7), channel_id=1, source_target_pairs={{8,0},{12,4},{16,8},{20,12},{24,16},{28,20},{32,24},{36,28},{40,32... | collective-permute-start | bytes 24584 | tf_op jit(solution)/shard_map/ppermute | solution.py:12
  115.6 11.9 %all_gather.11 = bf16[64,8,32]{0,1,2:T(8,128)(2,1)S(1)} all-gather(bf16[64,8,8]{0,1,2:T(8,128)(2,1)S(1)} %select_bitcast_fusion.6), channel_id=1, replica_groups=mesh['dom'=128,'sub'=4] {'sub'}, dimensions={2}, use_global_device_ids=true | all-gather | bytes 40960 | tf_op jit(solution)/shard_map/all_gather | solution.py:64
  128.5 0.7 gather_fusion.30
  129.2 0.7 gather_fusion.29
  129.9 0.7 gather_fusion.32
  130.6 0.7 gather_fusion.31
  131.3 0.7 gather_fusion.34
  132.0 0.7 gather_fusion.33
  137.9 3.1 %collective-permute-start.12 = (bf16[64,8,16]{2,0,1:T(8,128)(2,1)S(1)}, bf16[64,8,16]{2,0,1:T(8,128)(2,1)S(1)}, u32[]{:S(2)}, u32[]{:S(2)}) collective-permute-start(bf16[64,8,16]{2,0,1:T(8,128)(2,1)S(1)} %fusion.32), channel_id=1, source_target_pairs={{0,1},{1,0},{2,3},{3,2},{4,5},{5,4},{6,7},{7,6},{8,9},{9,8},{10,11... | collective-permute-start | bytes 49160 | tf_op jit(solution)/shard_map/ppermute | solution.py:22
  140.9 0.9 copy.358
  141.8 2.9 %collective-permute-done.12 = bf16[64,8,16]{2,0,1:T(8,128)(2,1)S(1)} collective-permute-done((bf16[64,8,16]{2,0,1:T(8,128)(2,1)S(1)}, bf16[64,8,16]{2,0,1:T(8,128)(2,1)S(1)}, u32[]{:S(2)}, u32[]{:S(2)}) %collective-permute-start.12) | collective-permute-done | bytes 16416 | tf_op jit(solution)/shard_map/ppermute | solution.py:22
  145.1 0.8 gather_fusion.1
  146.3 0.9 copy.357
  (225 shorter events, 27.2 us)
Async XLA Ops:
  0.6 145.4 %copy-start = (bf16[64,64]{1,0:T(8,128)(2,1)S(1)}, bf16[64,64]{1,0:T(8,128)(2,1)}, u32[]{:S(2)}) copy-start(bf16[64,64]{1,0:T(8,128)(2,1)} %param.25) | copy-start | bytes 24580
  0.6 1.9 %copy-start.8 = (s32[2,32]{1,0:T(2,128)S(1)}, s32[2,32]{1,0:T(2,128)}, u32[]{:S(2)}) copy-start(s32[2,32]{1,0:T(2,128)} %param.29) | copy-start | bytes 772
  3.2 9.9 %copy-start.9 = (s32[2,8]{1,0:T(2,128)S(1)}, s32[2,8]{1,0:T(2,128)}, u32[]{:S(2)}) copy-start(s32[2,8]{1,0:T(2,128)} %param.30) | copy-start | bytes 196
  3.3 34.9 %collective-permute-start = (bf16[64,8,32]{2,0,1:T(8,128)(2,1)S(1)}, bf16[64,8,32]{2,0,1:T(8,128)(2,1)S(1)}, u32[]{:S(2)}, u32[]{:S(2)}) collective-permute-start(bf16[64,8,32]{2,0,1:T(8,128)(2,1)S(1)} %select_bitcast_fusion.5), channel_id=1, source_target_pairs={{0,4},{4,8},{8,12},{12,16},{16,20},{20,24},{24,28},{28,32},{32,36}... | collective-permute-start | bytes 98312 | tf_op jit(solution)/shard_map/ppermute | solution.py:12
  5.9 17.7 %copy-start.10 = (s32[8]{0:T(128)S(1)}, s32[8]{0:T(128)}, u32[]{:S(2)}) copy-start(s32[8]{0:T(128)} %param.31) | copy-start | bytes 100
  5.9 17.7 %copy-start.11 = (s32[16]{0:T(128)S(1)}, s32[16]{0:T(128)}, u32[]{:S(2)}) copy-start(s32[16]{0:T(128)} %param.33) | copy-start | bytes 196
  5.9 17.7 %copy-start.12 = (s32[128]{0:T(128)S(1)}, s32[128]{0:T(128)}, u32[]{:S(2)}) copy-start(s32[128]{0:T(128)} %param.32) | copy-start | bytes 1540
  6.1 32.2 %collective-permute-start.1 = (bf16[64,8,32]{2,0,1:T(8,128)(2,1)S(1)}, bf16[64,8,32]{2,0,1:T(8,128)(2,1)S(1)}, u32[]{:S(2)}, u32[]{:S(2)}) collective-permute-start(bf16[64,8,32]{2,0,1:T(8,128)(2,1)S(1)} %select_bitcast_fusion.4), channel_id=1, source_target_pairs={{4,0},{8,4},{12,8},{16,12},{20,16},{24,20},{28,24},{32,28},{36,32}... | collective-permute-start | bytes 98312 | tf_op jit(solution)/shard_map/ppermute | solution.py:12
  13.7 24.2 %collective-permute-start.2 = (bf16[64,8,8]{0,1,2:T(8,128)(2,1)S(1)}, bf16[64,8,8]{0,1,2:T(8,128)(2,1)S(1)}, u32[]{:S(2)}, u32[]{:S(2)}) collective-permute-start(bf16[64,8,8]{0,1,2:T(8,128)(2,1)S(1)} %select_bitcast_fusion.14), channel_id=1, source_target_pairs={{0,8},{4,12},{8,16},{12,20},{16,24},{20,28},{24,32},{28,36},{32,40... | collective-permute-start | bytes 24584 | tf_op jit(solution)/shard_map/ppermute | solution.py:12
  16.3 21.8 %collective-permute-start.3 = (bf16[64,8,8]{0,1,2:T(8,128)(2,1)S(1)}, bf16[64,8,8]{0,1,2:T(8,128)(2,1)S(1)}, u32[]{:S(2)}, u32[]{:S(2)}) collective-permute-start(bf16[64,8,8]{0,1,2:T(8,128)(2,1)S(1)} %select_bitcast_fusion.13), channel_id=1, source_target_pairs={{8,0},{12,4},{16,8},{20,12},{24,16},{28,20},{32,24},{36,28},{40,32... | collective-permute-start | bytes 24584 | tf_op jit(solution)/shard_map/ppermute | solution.py:12
  23.7 0.8 copy-start.4
  23.7 0.8 copy-start.6
  23.7 1.3 copy-start.7
  23.7 1.4 copy-start.3
  23.8 1.4 copy-start.5
  46.7 1.0 copy-start.1
  48.0 1.0 copy-start.2
  52.9 30.9 %collective-permute-start.4 = (bf16[64,8,32]{2,0,1:T(8,128)(2,1)S(1)}, bf16[64,8,32]{2,0,1:T(8,128)(2,1)S(1)}, u32[]{:S(2)}, u32[]{:S(2)}) collective-permute-start(bf16[64,8,32]{2,0,1:T(8,128)(2,1)S(1)} %select_bitcast_fusion.3), channel_id=1, source_target_pairs={{0,4},{4,8},{8,12},{12,16},{16,20},{20,24},{24,28},{28,32},{32,36}... | collective-permute-start | bytes 98312 | tf_op jit(solution)/shard_map/ppermute | solution.py:12
  55.0 28.9 %collective-permute-start.5 = (bf16[64,8,32]{2,0,1:T(8,128)(2,1)S(1)}, bf16[64,8,32]{2,0,1:T(8,128)(2,1)S(1)}, u32[]{:S(2)}, u32[]{:S(2)}) collective-permute-start(bf16[64,8,32]{2,0,1:T(8,128)(2,1)S(1)} %select_bitcast_fusion.2), channel_id=1, source_target_pairs={{4,0},{8,4},{12,8},{16,12},{20,16},{24,20},{28,24},{32,28},{36,32}... | collective-permute-start | bytes 98312 | tf_op jit(solution)/shard_map/ppermute | solution.py:12
  62.1 21.5 %collective-permute-start.6 = (bf16[64,8,8]{0,1,2:T(8,128)(2,1)S(1)}, bf16[64,8,8]{0,1,2:T(8,128)(2,1)S(1)}, u32[]{:S(2)}, u32[]{:S(2)}) collective-permute-start(bf16[64,8,8]{0,1,2:T(8,128)(2,1)S(1)} %select_bitcast_fusion.11), channel_id=1, source_target_pairs={{0,8},{4,12},{8,16},{12,20},{16,24},{20,28},{24,32},{28,36},{32,40... | collective-permute-start | bytes 24584 | tf_op jit(solution)/shard_map/ppermute | solution.py:12
  64.1 19.6 %collective-permute-start.7 = (bf16[64,8,8]{0,1,2:T(8,128)(2,1)S(1)}, bf16[64,8,8]{0,1,2:T(8,128)(2,1)S(1)}, u32[]{:S(2)}, u32[]{:S(2)}) collective-permute-start(bf16[64,8,8]{0,1,2:T(8,128)(2,1)S(1)} %select_bitcast_fusion.10), channel_id=1, source_target_pairs={{8,0},{12,4},{16,8},{20,12},{24,16},{28,20},{32,24},{36,28},{40,32... | collective-permute-start | bytes 24584 | tf_op jit(solution)/shard_map/ppermute | solution.py:12
  97.1 30.8 %collective-permute-start.8 = (bf16[64,8,32]{2,0,1:T(8,128)(2,1)S(1)}, bf16[64,8,32]{2,0,1:T(8,128)(2,1)S(1)}, u32[]{:S(2)}, u32[]{:S(2)}) collective-permute-start(bf16[64,8,32]{2,0,1:T(8,128)(2,1)S(1)} %select_bitcast_fusion.1), channel_id=1, source_target_pairs={{0,4},{4,8},{8,12},{12,16},{16,20},{20,24},{24,28},{28,32},{32,36}... | collective-permute-start | bytes 98312 | tf_op jit(solution)/shard_map/ppermute | solution.py:12
  99.2 28.7 %collective-permute-start.9 = (bf16[64,8,32]{2,0,1:T(8,128)(2,1)S(1)}, bf16[64,8,32]{2,0,1:T(8,128)(2,1)S(1)}, u32[]{:S(2)}, u32[]{:S(2)}) collective-permute-start(bf16[64,8,32]{2,0,1:T(8,128)(2,1)S(1)} %select_bitcast_fusion), channel_id=1, source_target_pairs={{4,0},{8,4},{12,8},{16,12},{20,16},{24,20},{28,24},{32,28},{36,32}... | collective-permute-start | bytes 98312 | tf_op jit(solution)/shard_map/ppermute | solution.py:12
  106.3 21.3 %collective-permute-start.10 = (bf16[64,8,8]{0,1,2:T(8,128)(2,1)S(1)}, bf16[64,8,8]{0,1,2:T(8,128)(2,1)S(1)}, u32[]{:S(2)}, u32[]{:S(2)}) collective-permute-start(bf16[64,8,8]{0,1,2:T(8,128)(2,1)S(1)} %select_bitcast_fusion.8), channel_id=1, source_target_pairs={{0,8},{4,12},{8,16},{12,20},{16,24},{20,28},{24,32},{28,36},{32,40... | collective-permute-start | bytes 24584 | tf_op jit(solution)/shard_map/ppermute | solution.py:12
  108.3 19.5 %collective-permute-start.11 = (bf16[64,8,8]{0,1,2:T(8,128)(2,1)S(1)}, bf16[64,8,8]{0,1,2:T(8,128)(2,1)S(1)}, u32[]{:S(2)}, u32[]{:S(2)}) collective-permute-start(bf16[64,8,8]{0,1,2:T(8,128)(2,1)S(1)} %select_bitcast_fusion.7), channel_id=1, source_target_pairs={{8,0},{12,4},{16,8},{20,12},{24,16},{28,20},{32,24},{36,28},{40,32... | collective-permute-start | bytes 24584 | tf_op jit(solution)/shard_map/ppermute | solution.py:12
  137.9 6.9 %collective-permute-start.12 = (bf16[64,8,16]{2,0,1:T(8,128)(2,1)S(1)}, bf16[64,8,16]{2,0,1:T(8,128)(2,1)S(1)}, u32[]{:S(2)}, u32[]{:S(2)}) collective-permute-start(bf16[64,8,16]{2,0,1:T(8,128)(2,1)S(1)} %fusion.32), channel_id=1, source_target_pairs={{0,1},{1,0},{2,3},{3,2},{4,5},{5,4},{6,7},{7,6},{8,9},{9,8},{10,11... | collective-permute-start | bytes 49160 | tf_op jit(solution)/shard_map/ppermute | solution.py:22
where the time goes:
time: 148 us; the launch traced here: 147 us
  starting transfers between devices  57.2 us (39%)
  local copies, waits for them, and re-layouts  39 us (26%)
  blocking collectives  36.1 us (24%)
  matrix products  6.08 us (4%)
  other arithmetic  3.72 us (3%)
  waiting for transfers between devices  2.94 us (2%)
  between operations  2.13 us (1%)
    ppermute x12, starting transfers between devices, from_behind(): return lax.ppermute(array, axis, pairs)  54.1 us
    all_gather x3, blocking collectives, apply_local(): lax.all_gather(jnp.take(field_b, sub_send, axis=2), 'sub', axis=2, tiled=...  36.1 us
    gather x36, local copies, waits for them, and re-layouts, apply_local(): beside = jnp.take(extended, neighbours[face_index], axis=2)  16.1 us
    dot_general x23, matrix products, stack_apply(): product = jnp.dot(wide_blocks, operand, preferred_element_type=jnp.float32)  5.91 us
    concatenate x23, local copies, waits for them, and re-layouts, stack_apply(): jnp.concatenate(pieces, axis=0)  4.08 us
    unnamed x28, local copies, waits for them, and re-layouts  3.7 us
    ppermute x1, starting transfers between devices, partner_2(): return lax.ppermute(block, axis, route)  3.07 us
  transfers between devices with their start and end apart: 13, of which 1 were waited for; matrix products, arithmetic and copies ran while one was open for 4% of the time, Pallas kernels for 0%

commit v1 on v0

--- a/solution.py
+++ b/solution.py
@@ -61,7 +61,26 @@
         from_above = from_behind(down_near, "dom", -1)
         far_below = from_behind(up_far, "dom", 2)
         far_above = from_behind(down_far, "dom", -2)
-        side_rows = lax.all_gather(jnp.take(field_b, sub_send, axis=2), "sub", axis=2, tiled=True)
+        value = jnp.take(field_b, sub_send, axis=2)
+        length, mine, width = (lax.axis_size("sub"), lax.axis_index("sub"), value.shape[2])
+        right = [(i_2, (i_2 + 1) % length) for i_2 in range(length)]
+        downward = [(i_2, (i_2 - 1) % length) for i_2 in range(length)]
+        side_rows = jnp.zeros(
+            (*value.shape[:2], length * width, *value.shape[2 + 1 :]), value.dtype
+        )
+        side_rows = lax.dynamic_update_slice_in_dim(side_rows, value, mine * width, axis=2)
+        from_left = from_right = value
+        middle = length // 2
+        for step in range(1, middle + 1):
+            from_left = lax.ppermute(from_left, "sub", right)
+            side_rows = lax.dynamic_update_slice_in_dim(
+                side_rows, from_left, (mine - step) % length * width, axis=2
+            )
+            if step < length - middle:
+                from_right = lax.ppermute(from_right, "sub", downward)
+                side_rows = lax.dynamic_update_slice_in_dim(
+                    side_rows, from_right, (mine + step) % length * width, axis=2
+                )
         extended = jnp.concatenate(
             [field_b, from_below, from_above, far_below, far_above, side_rows], axis=2
         )

time: 148 us -> 160 us (1.081)
  the two profiles are of different devices: /device:TPU:256 before, /device:TPU:262 now
where the time goes in v1:
time: 160 us; the launch traced here: 159 us
  starting transfers between devices  84.9 us (53%)
  local copies, waits for them, and re-layouts  57.3 us (36%)
  matrix products  6.08 us (4%)
  other arithmetic  5.04 us (3%)
  waiting for transfers between devices  3.56 us (2%)
  between operations  2.45 us (2%)
    ppermute x12, starting transfers between devices, from_behind(): return lax.ppermute(array, axis, pairs)  54.1 us
    ppermute x6, starting transfers between devices, apply_local(): from_left = lax.ppermute(from_left, 'sub', right)  17.5 us
    gather x36, local copies, waits for them, and re-layouts, apply_local(): beside = jnp.take(extended, neighbours[face_index], axis=2)  16 us
    ppermute x3, starting transfers between devices, apply_local(): from_right = lax.ppermute(from_right, 'sub', downward)  10.8 us
    dynamic_update_slice x6, local copies, waits for them, and re-layouts, apply_local(): lax.dynamic_update_slice_in_dim(side_rows, from_left, (mine - step) % len...  10.5 us
    dot_general x23, matrix products, stack_apply(): product = jnp.dot(wide_blocks, operand, preferred_element_type=jnp.float32)  5.91 us
    dynamic_update_slice x3, local copies, waits for them, and re-layouts, apply_local(): lax.dynamic_update_slice_in_dim(side_rows, value, mine * width, axis=2)  5.25 us
    concatenate x23, local copies, waits for them, and re-layouts, stack_apply(): jnp.concatenate(pieces, axis=0)  4.08 us
  transfers between devices with their start and end apart: 22, of which 1 were waited for; matrix products, arithmetic and copies ran while one was open for 16% of the time, Pallas kernels for 0%

profile of v1, /device:TPU:262, one launch (start us, length us, event | category | flops | bytes accessed | tf_op | source)
XLA Modules:
  0.0 159.4 jit_solution(13728540013435692968)
XLA Ops:
  2.6 1.0 broadcast_select_fusion.27
  4.5 2.4 %collective-permute-start.4 = (bf16[64,8,8]{0,1,2:T(8,128)(2,1)S(1)}, bf16[64,8,8]{0,1,2:T(8,128)(2,1)S(1)}, u32[]{:S(2)}, u32[]{:S(2)}) collective-permute-start(bf16[64,8,8]{0,1,2:T(8,128)(2,1)S(1)} %select_bitcast_fusion.12), channel_id=1, source_target_pairs={{0,1},{1,2},{2,3},{3,0},{4,5},{5,6},{6,7},{7,4},{8,9},{9,10},{10,1... | collective-permute-start | bytes 24584 | tf_op jit(solution)/shard_map/ppermute | solution.py:75
  6.9 3.5 %collective-permute-start.5 = (bf16[64,8,8]{0,1,2:T(8,128)(2,1)S(1)}, bf16[64,8,8]{0,1,2:T(8,128)(2,1)S(1)}, u32[]{:S(2)}, u32[]{:S(2)}) collective-permute-start(bf16[64,8,8]{0,1,2:T(8,128)(2,1)S(1)} %select_bitcast_fusion.12), channel_id=1, source_target_pairs={{0,3},{1,0},{2,1},{3,2},{4,7},{5,4},{6,5},{7,6},{8,11},{9,8},{10,9... | collective-permute-start | bytes 24584 | tf_op jit(solution)/shard_map/ppermute | solution.py:80
  11.2 1.9 %collective-permute-start = (bf16[64,8,32]{2,0,1:T(8,128)(2,1)S(1)}, bf16[64,8,32]{2,0,1:T(8,128)(2,1)S(1)}, u32[]{:S(2)}, u32[]{:S(2)}) collective-permute-start(bf16[64,8,32]{2,0,1:T(8,128)(2,1)S(1)} %select_bitcast_fusion.5), channel_id=1, source_target_pairs={{0,4},{4,8},{8,12},{12,16},{16,20},{20,24},{24,28},{28,32},{32,36}... | collective-permute-start | bytes 98312 | tf_op jit(solution)/shard_map/ppermute | solution.py:12
  13.9 7.0 %collective-permute-start.1 = (bf16[64,8,32]{2,0,1:T(8,128)(2,1)S(1)}, bf16[64,8,32]{2,0,1:T(8,128)(2,1)S(1)}, u32[]{:S(2)}, u32[]{:S(2)}) collective-permute-start(bf16[64,8,32]{2,0,1:T(8,128)(2,1)S(1)} %select_bitcast_fusion.4), channel_id=1, source_target_pairs={{4,0},{8,4},{12,8},{16,12},{20,16},{24,20},{28,24},{32,28},{36,32}... | collective-permute-start | bytes 98312 | tf_op jit(solution)/shard_map/ppermute | solution.py:12
  21.5 1.9 %collective-permute-start.2 = (bf16[64,8,8]{0,1,2:T(8,128)(2,1)S(1)}, bf16[64,8,8]{0,1,2:T(8,128)(2,1)S(1)}, u32[]{:S(2)}, u32[]{:S(2)}) collective-permute-start(bf16[64,8,8]{0,1,2:T(8,128)(2,1)S(1)} %select_bitcast_fusion.14), channel_id=1, source_target_pairs={{0,8},{4,12},{8,16},{12,20},{16,24},{20,28},{24,32},{28,36},{32,40... | collective-permute-start | bytes 24584 | tf_op jit(solution)/shard_map/ppermute | solution.py:12
  25.4 7.2 %collective-permute-start.3 = (bf16[64,8,8]{0,1,2:T(8,128)(2,1)S(1)}, bf16[64,8,8]{0,1,2:T(8,128)(2,1)S(1)}, u32[]{:S(2)}, u32[]{:S(2)}) collective-permute-start(bf16[64,8,8]{0,1,2:T(8,128)(2,1)S(1)} %select_bitcast_fusion.13), channel_id=1, source_target_pairs={{8,0},{12,4},{16,8},{20,12},{24,16},{28,20},{32,24},{36,28},{40,32... | collective-permute-start | bytes 24584 | tf_op jit(solution)/shard_map/ppermute | solution.py:12
  32.7 3.6 %collective-permute-start.6 = (bf16[64,8,8]{0,1,2:T(8,128)(2,1)S(1)}, bf16[64,8,8]{0,1,2:T(8,128)(2,1)S(1)}, u32[]{:S(2)}, u32[]{:S(2)}) collective-permute-start(bf16[64,8,8]{0,1,2:T(8,128)(2,1)S(1)} %collective-permute-done.4), channel_id=1, source_target_pairs={{0,1},{1,2},{2,3},{3,0},{4,5},{5,6},{6,7},{7,4},{8,9},{9,10},{10,1... | collective-permute-start | bytes 24584 | tf_op jit(solution)/shard_map/ppermute | solution.py:75
  36.5 1.8 %dynamic_update_slice.36 = bf16[64,8,32]{2,0,1:T(8,128)(2,1)S(1)} dynamic-update-slice(bf16[64,8,32]{2,0,1:T(8,128)(2,1)S(1)} %broadcast.134.clone, bf16[64,8,8]{2,0,1:T(8,128)(2,1)S(1)} %copy.152, s32[]{:T(128)} %constant.98.clone.1, s32[]{:T(128)} %constant.98.clone.1, s32[]{:T(128)S(6)} %select_n.226) | dynamic-update-slice | bytes 16388 | tf_op jit(solution)/shard_map/dynamic_update_slice | solution.py:71
  38.4 1.8 %dynamic_update_slice.37 = bf16[64,8,32]{2,0,1:T(8,128)(2,1)S(1)} dynamic-update-slice(bf16[64,8,32]{2,0,1:T(8,128)(2,1)S(1)} %dynamic_update_slice.36, bf16[64,8,8]{2,0,1:T(8,128)(2,1)S(1)} %copy.153, s32[]{:T(128)} %constant.98.clone.1, s32[]{:T(128)} %constant.98.clone.1, s32[]{:T(128)S(6)} %select_n.228) | dynamic-update-slice | bytes 16388 | tf_op jit(solution)/shard_map/dynamic_update_slice | solution.py:76
  41.2 1.8 %dynamic_update_slice.39 = bf16[64,8,32]{2,0,1:T(8,128)(2,1)S(1)} dynamic-update-slice(bf16[64,8,32]{2,0,1:T(8,128)(2,1)S(1)} %dynamic_update_slice.38, bf16[64,8,8]{2,0,1:T(8,128)(2,1)S(1)} %copy.155, s32[]{:T(128)} %constant.98.clone.1, s32[]{:T(128)} %constant.98.clone.1, s32[]{:T(128)S(6)} %select_n.232) | dynamic-update-slice | bytes 16388 | tf_op jit(solution)/shard_map/dynamic_update_slice | solution.py:76
  44.7 0.7 gather_fusion.8
  45.9 0.7 gather_fusion.9
  47.0 0.7 gather_fusion.10
  48.2 0.7 gather_fusion.11
  49.3 0.7 gather_fusion.12
  53.0 0.7 copy-done.2
  57.2 2.2 %collective-permute-start.11 = (bf16[64,8,8]{0,1,2:T(8,128)(2,1)S(1)}, bf16[64,8,8]{0,1,2:T(8,128)(2,1)S(1)}, u32[]{:S(2)}, u32[]{:S(2)}) collective-permute-start(bf16[64,8,8]{0,1,2:T(8,128)(2,1)S(1)} %select_bitcast_fusion.9), channel_id=1, source_target_pairs={{0,1},{1,2},{2,3},{3,0},{4,5},{5,6},{6,7},{7,4},{8,9},{9,10},{10,1... | collective-permute-start | bytes 24584 | tf_op jit(solution)/shard_map/ppermute | solution.py:75
  59.4 3.6 %collective-permute-start.12 = (bf16[64,8,8]{0,1,2:T(8,128)(2,1)S(1)}, bf16[64,8,8]{0,1,2:T(8,128)(2,1)S(1)}, u32[]{:S(2)}, u32[]{:S(2)}) collective-permute-start(bf16[64,8,8]{0,1,2:T(8,128)(2,1)S(1)} %select_bitcast_fusion.9), channel_id=1, source_target_pairs={{0,3},{1,0},{2,1},{3,2},{4,7},{5,4},{6,5},{7,6},{8,11},{9,8},{10,9... | collective-permute-start | bytes 24584 | tf_op jit(solution)/shard_map/ppermute | solution.py:80
  63.2 1.9 %collective-permute-start.7 = (bf16[64,8,32]{2,0,1:T(8,128)(2,1)S(1)}, bf16[64,8,32]{2,0,1:T(8,128)(2,1)S(1)}, u32[]{:S(2)}, u32[]{:S(2)}) collective-permute-start(bf16[64,8,32]{2,0,1:T(8,128)(2,1)S(1)} %select_bitcast_fusion.3), channel_id=1, source_target_pairs={{0,4},{4,8},{8,12},{12,16},{16,20},{20,24},{24,28},{28,32},{32,36}... | collective-permute-start | bytes 98312 | tf_op jit(solution)/shard_map/ppermute | solution.py:12
  65.3 7.0 %collective-permute-start.8 = (bf16[64,8,32]{2,0,1:T(8,128)(2,1)S(1)}, bf16[64,8,32]{2,0,1:T(8,128)(2,1)S(1)}, u32[]{:S(2)}, u32[]{:S(2)}) collective-permute-start(bf16[64,8,32]{2,0,1:T(8,128)(2,1)S(1)} %select_bitcast_fusion.2), channel_id=1, source_target_pairs={{4,0},{8,4},{12,8},{16,12},{20,16},{24,20},{28,24},{32,28},{36,32}... | collective-permute-start | bytes 98312 | tf_op jit(solution)/shard_map/ppermute | solution.py:12
  72.6 1.9 %collective-permute-start.9 = (bf16[64,8,8]{0,1,2:T(8,128)(2,1)S(1)}, bf16[64,8,8]{0,1,2:T(8,128)(2,1)S(1)}, u32[]{:S(2)}, u32[]{:S(2)}) collective-permute-start(bf16[64,8,8]{0,1,2:T(8,128)(2,1)S(1)} %select_bitcast_fusion.11), channel_id=1, source_target_pairs={{0,8},{4,12},{8,16},{12,20},{16,24},{20,28},{24,32},{28,36},{32,40... | collective-permute-start | bytes 24584 | tf_op jit(solution)/shard_map/ppermute | solution.py:12
  74.5 7.2 %collective-permute-start.10 = (bf16[64,8,8]{0,1,2:T(8,128)(2,1)S(1)}, bf16[64,8,8]{0,1,2:T(8,128)(2,1)S(1)}, u32[]{:S(2)}, u32[]{:S(2)}) collective-permute-start(bf16[64,8,8]{0,1,2:T(8,128)(2,1)S(1)} %select_bitcast_fusion.10), channel_id=1, source_target_pairs={{8,0},{12,4},{16,8},{20,12},{24,16},{28,20},{32,24},{36,28},{40,32... | collective-permute-start | bytes 24584 | tf_op jit(solution)/shard_map/ppermute | solution.py:12
  81.8 3.6 %collective-permute-start.13 = (bf16[64,8,8]{0,1,2:T(8,128)(2,1)S(1)}, bf16[64,8,8]{0,1,2:T(8,128)(2,1)S(1)}, u32[]{:S(2)}, u32[]{:S(2)}) collective-permute-start(bf16[64,8,8]{0,1,2:T(8,128)(2,1)S(1)} %collective-permute-done.11), channel_id=1, source_target_pairs={{0,1},{1,2},{2,3},{3,0},{4,5},{5,6},{6,7},{7,4},{8,9},{9,10},{10,1... | collective-permute-start | bytes 24584 | tf_op jit(solution)/shard_map/ppermute | solution.py:75
  85.8 1.8 %dynamic_update_slice.40 = bf16[64,8,32]{2,0,1:T(8,128)(2,1)S(1)} dynamic-update-slice(bf16[64,8,32]{2,0,1:T(8,128)(2,1)S(1)} %broadcast.134.clone.1, bf16[64,8,8]{2,0,1:T(8,128)(2,1)S(1)} %copy.187, s32[]{:T(128)} %constant.98.clone.1, s32[]{:T(128)} %constant.98.clone.1, s32[]{:T(128)S(6)} %select_n.226) | dynamic-update-slice | bytes 16388 | tf_op jit(solution)/shard_map/dynamic_update_slice | solution.py:71
  87.7 1.8 %dynamic_update_slice.41 = bf16[64,8,32]{2,0,1:T(8,128)(2,1)S(1)} dynamic-update-slice(bf16[64,8,32]{2,0,1:T(8,128)(2,1)S(1)} %dynamic_update_slice.40, bf16[64,8,8]{2,0,1:T(8,128)(2,1)S(1)} %copy.188, s32[]{:T(128)} %constant.98.clone.1, s32[]{:T(128)} %constant.98.clone.1, s32[]{:T(128)S(6)} %select_n.228) | dynamic-update-slice | bytes 16388 | tf_op jit(solution)/shard_map/dynamic_update_slice | solution.py:76
  90.5 1.8 %dynamic_update_slice.43 = bf16[64,8,32]{2,0,1:T(8,128)(2,1)S(1)} dynamic-update-slice(bf16[64,8,32]{2,0,1:T(8,128)(2,1)S(1)} %dynamic_update_slice.42, bf16[64,8,8]{2,0,1:T(8,128)(2,1)S(1)} %copy.190, s32[]{:T(128)} %constant.98.clone.1, s32[]{:T(128)} %constant.98.clone.1, s32[]{:T(128)S(6)} %select_n.232) | dynamic-update-slice | bytes 16388 | tf_op jit(solution)/shard_map/dynamic_update_slice | solution.py:76
  94.3 0.7 gather_fusion.20
  95.0 0.7 gather_fusion.21
  95.7 0.7 gather_fusion.22
  105.0 2.2 %collective-permute-start.18 = (bf16[64,8,8]{0,1,2:T(8,128)(2,1)S(1)}, bf16[64,8,8]{0,1,2:T(8,128)(2,1)S(1)}, u32[]{:S(2)}, u32[]{:S(2)}) collective-permute-start(bf16[64,8,8]{0,1,2:T(8,128)(2,1)S(1)} %select_bitcast_fusion.6), channel_id=1, source_target_pairs={{0,1},{1,2},{2,3},{3,0},{4,5},{5,6},{6,7},{7,4},{8,9},{9,10},{10,1... | collective-permute-start | bytes 24584 | tf_op jit(solution)/shard_map/ppermute | solution.py:75
  107.2 3.7 %collective-permute-start.19 = (bf16[64,8,8]{0,1,2:T(8,128)(2,1)S(1)}, bf16[64,8,8]{0,1,2:T(8,128)(2,1)S(1)}, u32[]{:S(2)}, u32[]{:S(2)}) collective-permute-start(bf16[64,8,8]{0,1,2:T(8,128)(2,1)S(1)} %select_bitcast_fusion.6), channel_id=1, source_target_pairs={{0,3},{1,0},{2,1},{3,2},{4,7},{5,4},{6,5},{7,6},{8,11},{9,8},{10,9... | collective-permute-start | bytes 24584 | tf_op jit(solution)/shard_map/ppermute | solution.py:80
  111.0 1.9 %collective-permute-start.14 = (bf16[64,8,32]{2,0,1:T(8,128)(2,1)S(1)}, bf16[64,8,32]{2,0,1:T(8,128)(2,1)S(1)}, u32[]{:S(2)}, u32[]{:S(2)}) collective-permute-start(bf16[64,8,32]{2,0,1:T(8,128)(2,1)S(1)} %select_bitcast_fusion.1), channel_id=1, source_target_pairs={{0,4},{4,8},{8,12},{12,16},{16,20},{20,24},{24,28},{28,32},{32,36}... | collective-permute-start | bytes 98312 | tf_op jit(solution)/shard_map/ppermute | solution.py:12
  113.1 7.0 %collective-permute-start.15 = (bf16[64,8,32]{2,0,1:T(8,128)(2,1)S(1)}, bf16[64,8,32]{2,0,1:T(8,128)(2,1)S(1)}, u32[]{:S(2)}, u32[]{:S(2)}) collective-permute-start(bf16[64,8,32]{2,0,1:T(8,128)(2,1)S(1)} %select_bitcast_fusion), channel_id=1, source_target_pairs={{4,0},{8,4},{12,8},{16,12},{20,16},{24,20},{28,24},{32,28},{36,32}... | collective-permute-start | bytes 98312 | tf_op jit(solution)/shard_map/ppermute | solution.py:12
  120.4 1.9 %collective-permute-start.16 = (bf16[64,8,8]{0,1,2:T(8,128)(2,1)S(1)}, bf16[64,8,8]{0,1,2:T(8,128)(2,1)S(1)}, u32[]{:S(2)}, u32[]{:S(2)}) collective-permute-start(bf16[64,8,8]{0,1,2:T(8,128)(2,1)S(1)} %select_bitcast_fusion.8), channel_id=1, source_target_pairs={{0,8},{4,12},{8,16},{12,20},{16,24},{20,28},{24,32},{28,36},{32,40... | collective-permute-start | bytes 24584 | tf_op jit(solution)/shard_map/ppermute | solution.py:12
  122.4 7.2 %collective-permute-start.17 = (bf16[64,8,8]{0,1,2:T(8,128)(2,1)S(1)}, bf16[64,8,8]{0,1,2:T(8,128)(2,1)S(1)}, u32[]{:S(2)}, u32[]{:S(2)}) collective-permute-start(bf16[64,8,8]{0,1,2:T(8,128)(2,1)S(1)} %select_bitcast_fusion.7), channel_id=1, source_target_pairs={{8,0},{12,4},{16,8},{20,12},{24,16},{28,20},{32,24},{36,28},{40,32... | collective-permute-start | bytes 24584 | tf_op jit(solution)/shard_map/ppermute | solution.py:12
  129.6 3.6 %collective-permute-start.20 = (bf16[64,8,8]{0,1,2:T(8,128)(2,1)S(1)}, bf16[64,8,8]{0,1,2:T(8,128)(2,1)S(1)}, u32[]{:S(2)}, u32[]{:S(2)}) collective-permute-start(bf16[64,8,8]{0,1,2:T(8,128)(2,1)S(1)} %collective-permute-done.18), channel_id=1, source_target_pairs={{0,1},{1,2},{2,3},{3,0},{4,5},{5,6},{6,7},{7,4},{8,9},{9,10},{10,1... | collective-permute-start | bytes 24584 | tf_op jit(solution)/shard_map/ppermute | solution.py:75
  133.7 1.8 %dynamic_update_slice.44 = bf16[64,8,32]{2,0,1:T(8,128)(2,1)S(1)} dynamic-update-slice(bf16[64,8,32]{2,0,1:T(8,128)(2,1)S(1)} %broadcast.134, bf16[64,8,8]{2,0,1:T(8,128)(2,1)S(1)} %copy.221, s32[]{:T(128)} %constant.98.clone.1, s32[]{:T(128)} %constant.98.clone.1, s32[]{:T(128)S(6)} %select_n.226) | dynamic-update-slice | bytes 16388 | tf_op jit(solution)/shard_map/dynamic_update_slice | solution.py:71
  135.6 1.8 %dynamic_update_slice.45 = bf16[64,8,32]{2,0,1:T(8,128)(2,1)S(1)} dynamic-update-slice(bf16[64,8,32]{2,0,1:T(8,128)(2,1)S(1)} %dynamic_update_slice.44, bf16[64,8,8]{2,0,1:T(8,128)(2,1)S(1)} %copy.222, s32[]{:T(128)} %constant.98.clone.1, s32[]{:T(128)} %constant.98.clone.1, s32[]{:T(128)S(6)} %select_n.228) | dynamic-update-slice | bytes 16388 | tf_op jit(solution)/shard_map/dynamic_update_slice | solution.py:76
  138.4 1.8 %dynamic_update_slice.47 = bf16[64,8,32]{2,0,1:T(8,128)(2,1)S(1)} dynamic-update-slice(bf16[64,8,32]{2,0,1:T(8,128)(2,1)S(1)} %dynamic_update_slice.46, bf16[64,8,8]{2,0,1:T(8,128)(2,1)S(1)} %copy.224, s32[]{:T(128)} %constant.98.clone.1, s32[]{:T(128)} %constant.98.clone.1, s32[]{:T(128)S(6)} %select_n.232) | dynamic-update-slice | bytes 16388 | tf_op jit(solution)/shard_map/dynamic_update_slice | solution.py:76
  142.1 0.7 gather_fusion.32
  142.8 0.7 gather_fusion.31
  144.2 0.7 gather_fusion.33
  150.1 2.5 %collective-permute-start.21 = (bf16[64,8,16]{2,0,1:T(8,128)(2,1)S(1)}, bf16[64,8,16]{2,0,1:T(8,128)(2,1)S(1)}, u32[]{:S(2)}, u32[]{:S(2)}) collective-permute-start(bf16[64,8,16]{2,0,1:T(8,128)(2,1)S(1)} %fusion.32), channel_id=1, source_target_pairs={{0,1},{1,0},{2,3},{3,2},{4,5},{5,4},{6,7},{7,6},{8,9},{9,8},{10,11... | collective-permute-start | bytes 49160 | tf_op jit(solution)/shard_map/ppermute | solution.py:22
  152.6 0.9 copy.253
  153.4 3.5 %collective-permute-done.21 = bf16[64,8,16]{2,0,1:T(8,128)(2,1)S(1)} collective-permute-done((bf16[64,8,16]{2,0,1:T(8,128)(2,1)S(1)}, bf16[64,8,16]{2,0,1:T(8,128)(2,1)S(1)}, u32[]{:S(2)}, u32[]{:S(2)}) %collective-permute-start.21) | collective-permute-done | bytes 16416 | tf_op jit(solution)/shard_map/ppermute | solution.py:22
  157.3 0.8 gather_fusion.1
  158.5 0.9 copy.252
  (262 shorter events, 40.9 us)
Async XLA Ops:
  0.6 157.7 %copy-start = (bf16[64,64]{1,0:T(8,128)(2,1)S(1)}, bf16[64,64]{1,0:T(8,128)(2,1)}, u32[]{:S(2)}) copy-start(bf16[64,64]{1,0:T(8,128)(2,1)} %param.25) | copy-start | bytes 24580
  2.6 7.7 %copy-start.8 = (s32[2,32]{1,0:T(2,128)S(1)}, s32[2,32]{1,0:T(2,128)}, u32[]{:S(2)}) copy-start(s32[2,32]{1,0:T(2,128)} %param.29) | copy-start | bytes 772
  4.5 20.9 %collective-permute-start.4 = (bf16[64,8,8]{0,1,2:T(8,128)(2,1)S(1)}, bf16[64,8,8]{0,1,2:T(8,128)(2,1)S(1)}, u32[]{:S(2)}, u32[]{:S(2)}) collective-permute-start(bf16[64,8,8]{0,1,2:T(8,128)(2,1)S(1)} %select_bitcast_fusion.12), channel_id=1, source_target_pairs={{0,1},{1,2},{2,3},{3,0},{4,5},{5,6},{6,7},{7,4},{8,9},{9,10},{10,1... | collective-permute-start | bytes 24584 | tf_op jit(solution)/shard_map/ppermute | solution.py:75
  6.9 25.8 %collective-permute-start.5 = (bf16[64,8,8]{0,1,2:T(8,128)(2,1)S(1)}, bf16[64,8,8]{0,1,2:T(8,128)(2,1)S(1)}, u32[]{:S(2)}, u32[]{:S(2)}) collective-permute-start(bf16[64,8,8]{0,1,2:T(8,128)(2,1)S(1)} %select_bitcast_fusion.12), channel_id=1, source_target_pairs={{0,3},{1,0},{2,1},{3,2},{4,7},{5,4},{6,5},{7,6},{8,11},{9,8},{10,9... | collective-permute-start | bytes 24584 | tf_op jit(solution)/shard_map/ppermute | solution.py:80
  11.0 9.9 %copy-start.9 = (s32[2,8]{1,0:T(2,128)S(1)}, s32[2,8]{1,0:T(2,128)}, u32[]{:S(2)}) copy-start(s32[2,8]{1,0:T(2,128)} %param.30) | copy-start | bytes 196
  11.1 12.3 %copy-start.10 = (s32[16]{0:T(128)S(1)}, s32[16]{0:T(128)}, u32[]{:S(2)}) copy-start(s32[16]{0:T(128)} %param.33) | copy-start | bytes 196
  11.2 12.4 %copy-start.11 = (s32[128]{0:T(128)S(1)}, s32[128]{0:T(128)}, u32[]{:S(2)}) copy-start(s32[128]{0:T(128)} %param.32) | copy-start | bytes 1540
  11.2 31.8 %collective-permute-start = (bf16[64,8,32]{2,0,1:T(8,128)(2,1)S(1)}, bf16[64,8,32]{2,0,1:T(8,128)(2,1)S(1)}, u32[]{:S(2)}, u32[]{:S(2)}) collective-permute-start(bf16[64,8,32]{2,0,1:T(8,128)(2,1)S(1)} %select_bitcast_fusion.5), channel_id=1, source_target_pairs={{0,4},{4,8},{8,12},{12,16},{16,20},{20,24},{24,28},{28,32},{32,36}... | collective-permute-start | bytes 98312 | tf_op jit(solution)/shard_map/ppermute | solution.py:12
  13.9 29.1 %collective-permute-start.1 = (bf16[64,8,32]{2,0,1:T(8,128)(2,1)S(1)}, bf16[64,8,32]{2,0,1:T(8,128)(2,1)S(1)}, u32[]{:S(2)}, u32[]{:S(2)}) collective-permute-start(bf16[64,8,32]{2,0,1:T(8,128)(2,1)S(1)} %select_bitcast_fusion.4), channel_id=1, source_target_pairs={{4,0},{8,4},{12,8},{16,12},{20,16},{24,20},{28,24},{32,28},{36,32}... | collective-permute-start | bytes 98312 | tf_op jit(solution)/shard_map/ppermute | solution.py:12
  21.5 19.3 %collective-permute-start.2 = (bf16[64,8,8]{0,1,2:T(8,128)(2,1)S(1)}, bf16[64,8,8]{0,1,2:T(8,128)(2,1)S(1)}, u32[]{:S(2)}, u32[]{:S(2)}) collective-permute-start(bf16[64,8,8]{0,1,2:T(8,128)(2,1)S(1)} %select_bitcast_fusion.14), channel_id=1, source_target_pairs={{0,8},{4,12},{8,16},{12,20},{16,24},{20,28},{24,32},{28,36},{32,40... | collective-permute-start | bytes 24584 | tf_op jit(solution)/shard_map/ppermute | solution.py:12
  23.6 0.8 copy-start.4
  23.6 0.8 copy-start.6
  23.6 1.3 copy-start.7
  23.6 1.4 copy-start.3
  23.6 1.4 copy-start.5
  25.4 15.5 %collective-permute-start.3 = (bf16[64,8,8]{0,1,2:T(8,128)(2,1)S(1)}, bf16[64,8,8]{0,1,2:T(8,128)(2,1)S(1)}, u32[]{:S(2)}, u32[]{:S(2)}) collective-permute-start(bf16[64,8,8]{0,1,2:T(8,128)(2,1)S(1)} %select_bitcast_fusion.13), channel_id=1, source_target_pairs={{8,0},{12,4},{16,8},{20,12},{24,16},{28,20},{32,24},{36,28},{40,32... | collective-permute-start | bytes 24584 | tf_op jit(solution)/shard_map/ppermute | solution.py:12
  32.7 8.4 %collective-permute-start.6 = (bf16[64,8,8]{0,1,2:T(8,128)(2,1)S(1)}, bf16[64,8,8]{0,1,2:T(8,128)(2,1)S(1)}, u32[]{:S(2)}, u32[]{:S(2)}) collective-permute-start(bf16[64,8,8]{0,1,2:T(8,128)(2,1)S(1)} %collective-permute-done.4), channel_id=1, source_target_pairs={{0,1},{1,2},{2,3},{3,0},{4,5},{5,6},{6,7},{7,4},{8,9},{9,10},{10,1... | collective-permute-start | bytes 24584 | tf_op jit(solution)/shard_map/ppermute | solution.py:75
  51.5 1.0 copy-start.1
  52.7 1.0 copy-start.2
  57.2 17.4 %collective-permute-start.11 = (bf16[64,8,8]{0,1,2:T(8,128)(2,1)S(1)}, bf16[64,8,8]{0,1,2:T(8,128)(2,1)S(1)}, u32[]{:S(2)}, u32[]{:S(2)}) collective-permute-start(bf16[64,8,8]{0,1,2:T(8,128)(2,1)S(1)} %select_bitcast_fusion.9), channel_id=1, source_target_pairs={{0,1},{1,2},{2,3},{3,0},{4,5},{5,6},{6,7},{7,4},{8,9},{9,10},{10,1... | collective-permute-start | bytes 24584 | tf_op jit(solution)/shard_map/ppermute | solution.py:75
  59.4 22.4 %collective-permute-start.12 = (bf16[64,8,8]{0,1,2:T(8,128)(2,1)S(1)}, bf16[64,8,8]{0,1,2:T(8,128)(2,1)S(1)}, u32[]{:S(2)}, u32[]{:S(2)}) collective-permute-start(bf16[64,8,8]{0,1,2:T(8,128)(2,1)S(1)} %select_bitcast_fusion.9), channel_id=1, source_target_pairs={{0,3},{1,0},{2,1},{3,2},{4,7},{5,4},{6,5},{7,6},{8,11},{9,8},{10,9... | collective-permute-start | bytes 24584 | tf_op jit(solution)/shard_map/ppermute | solution.py:80
  63.2 29.1 %collective-permute-start.7 = (bf16[64,8,32]{2,0,1:T(8,128)(2,1)S(1)}, bf16[64,8,32]{2,0,1:T(8,128)(2,1)S(1)}, u32[]{:S(2)}, u32[]{:S(2)}) collective-permute-start(bf16[64,8,32]{2,0,1:T(8,128)(2,1)S(1)} %select_bitcast_fusion.3), channel_id=1, source_target_pairs={{0,4},{4,8},{8,12},{12,16},{16,20},{20,24},{24,28},{28,32},{32,36}... | collective-permute-start | bytes 98312 | tf_op jit(solution)/shard_map/ppermute | solution.py:12
  65.3 27.0 %collective-permute-start.8 = (bf16[64,8,32]{2,0,1:T(8,128)(2,1)S(1)}, bf16[64,8,32]{2,0,1:T(8,128)(2,1)S(1)}, u32[]{:S(2)}, u32[]{:S(2)}) collective-permute-start(bf16[64,8,32]{2,0,1:T(8,128)(2,1)S(1)} %select_bitcast_fusion.2), channel_id=1, source_target_pairs={{4,0},{8,4},{12,8},{16,12},{20,16},{24,20},{28,24},{32,28},{36,32}... | collective-permute-start | bytes 98312 | tf_op jit(solution)/shard_map/ppermute | solution.py:12
  72.6 17.5 %collective-permute-start.9 = (bf16[64,8,8]{0,1,2:T(8,128)(2,1)S(1)}, bf16[64,8,8]{0,1,2:T(8,128)(2,1)S(1)}, u32[]{:S(2)}, u32[]{:S(2)}) collective-permute-start(bf16[64,8,8]{0,1,2:T(8,128)(2,1)S(1)} %select_bitcast_fusion.11), channel_id=1, source_target_pairs={{0,8},{4,12},{8,16},{12,20},{16,24},{20,28},{24,32},{28,36},{32,40... | collective-permute-start | bytes 24584 | tf_op jit(solution)/shard_map/ppermute | solution.py:12
  74.5 15.7 %collective-permute-start.10 = (bf16[64,8,8]{0,1,2:T(8,128)(2,1)S(1)}, bf16[64,8,8]{0,1,2:T(8,128)(2,1)S(1)}, u32[]{:S(2)}, u32[]{:S(2)}) collective-permute-start(bf16[64,8,8]{0,1,2:T(8,128)(2,1)S(1)} %select_bitcast_fusion.10), channel_id=1, source_target_pairs={{8,0},{12,4},{16,8},{20,12},{24,16},{28,20},{32,24},{36,28},{40,32... | collective-permute-start | bytes 24584 | tf_op jit(solution)/shard_map/ppermute | solution.py:12
  81.8 8.6 %collective-permute-start.13 = (bf16[64,8,8]{0,1,2:T(8,128)(2,1)S(1)}, bf16[64,8,8]{0,1,2:T(8,128)(2,1)S(1)}, u32[]{:S(2)}, u32[]{:S(2)}) collective-permute-start(bf16[64,8,8]{0,1,2:T(8,128)(2,1)S(1)} %collective-permute-done.11), channel_id=1, source_target_pairs={{0,1},{1,2},{2,3},{3,0},{4,5},{5,6},{6,7},{7,4},{8,9},{9,10},{10,1... | collective-permute-start | bytes 24584 | tf_op jit(solution)/shard_map/ppermute | solution.py:75
  105.0 17.4 %collective-permute-start.18 = (bf16[64,8,8]{0,1,2:T(8,128)(2,1)S(1)}, bf16[64,8,8]{0,1,2:T(8,128)(2,1)S(1)}, u32[]{:S(2)}, u32[]{:S(2)}) collective-permute-start(bf16[64,8,8]{0,1,2:T(8,128)(2,1)S(1)} %select_bitcast_fusion.6), channel_id=1, source_target_pairs={{0,1},{1,2},{2,3},{3,0},{4,5},{5,6},{6,7},{7,4},{8,9},{9,10},{10,1... | collective-permute-start | bytes 24584 | tf_op jit(solution)/shard_map/ppermute | solution.py:75
  107.2 22.5 %collective-permute-start.19 = (bf16[64,8,8]{0,1,2:T(8,128)(2,1)S(1)}, bf16[64,8,8]{0,1,2:T(8,128)(2,1)S(1)}, u32[]{:S(2)}, u32[]{:S(2)}) collective-permute-start(bf16[64,8,8]{0,1,2:T(8,128)(2,1)S(1)} %select_bitcast_fusion.6), channel_id=1, source_target_pairs={{0,3},{1,0},{2,1},{3,2},{4,7},{5,4},{6,5},{7,6},{8,11},{9,8},{10,9... | collective-permute-start | bytes 24584 | tf_op jit(solution)/shard_map/ppermute | solution.py:80
  111.0 29.1 %collective-permute-start.14 = (bf16[64,8,32]{2,0,1:T(8,128)(2,1)S(1)}, bf16[64,8,32]{2,0,1:T(8,128)(2,1)S(1)}, u32[]{:S(2)}, u32[]{:S(2)}) collective-permute-start(bf16[64,8,32]{2,0,1:T(8,128)(2,1)S(1)} %select_bitcast_fusion.1), channel_id=1, source_target_pairs={{0,4},{4,8},{8,12},{12,16},{16,20},{20,24},{24,28},{28,32},{32,36}... | collective-permute-start | bytes 98312 | tf_op jit(solution)/shard_map/ppermute | solution.py:12
  113.1 27.0 %collective-permute-start.15 = (bf16[64,8,32]{2,0,1:T(8,128)(2,1)S(1)}, bf16[64,8,32]{2,0,1:T(8,128)(2,1)S(1)}, u32[]{:S(2)}, u32[]{:S(2)}) collective-permute-start(bf16[64,8,32]{2,0,1:T(8,128)(2,1)S(1)} %select_bitcast_fusion), channel_id=1, source_target_pairs={{4,0},{8,4},{12,8},{16,12},{20,16},{24,20},{28,24},{32,28},{36,32}... | collective-permute-start | bytes 98312 | tf_op jit(solution)/shard_map/ppermute | solution.py:12
  120.4 17.5 %collective-permute-start.16 = (bf16[64,8,8]{0,1,2:T(8,128)(2,1)S(1)}, bf16[64,8,8]{0,1,2:T(8,128)(2,1)S(1)}, u32[]{:S(2)}, u32[]{:S(2)}) collective-permute-start(bf16[64,8,8]{0,1,2:T(8,128)(2,1)S(1)} %select_bitcast_fusion.8), channel_id=1, source_target_pairs={{0,8},{4,12},{8,16},{12,20},{16,24},{20,28},{24,32},{28,36},{32,40... | collective-permute-start | bytes 24584 | tf_op jit(solution)/shard_map/ppermute | solution.py:12
  122.4 15.7 %collective-permute-start.17 = (bf16[64,8,8]{0,1,2:T(8,128)(2,1)S(1)}, bf16[64,8,8]{0,1,2:T(8,128)(2,1)S(1)}, u32[]{:S(2)}, u32[]{:S(2)}) collective-permute-start(bf16[64,8,8]{0,1,2:T(8,128)(2,1)S(1)} %select_bitcast_fusion.7), channel_id=1, source_target_pairs={{8,0},{12,4},{16,8},{20,12},{24,16},{28,20},{32,24},{36,28},{40,32... | collective-permute-start | bytes 24584 | tf_op jit(solution)/shard_map/ppermute | solution.py:12
  129.6 8.6 %collective-permute-start.20 = (bf16[64,8,8]{0,1,2:T(8,128)(2,1)S(1)}, bf16[64,8,8]{0,1,2:T(8,128)(2,1)S(1)}, u32[]{:S(2)}, u32[]{:S(2)}) collective-permute-start(bf16[64,8,8]{0,1,2:T(8,128)(2,1)S(1)} %collective-permute-done.18), channel_id=1, source_target_pairs={{0,1},{1,2},{2,3},{3,0},{4,5},{5,6},{6,7},{7,4},{8,9},{9,10},{10,1... | collective-permute-start | bytes 24584 | tf_op jit(solution)/shard_map/ppermute | solution.py:75
  150.1 6.9 %collective-permute-start.21 = (bf16[64,8,16]{2,0,1:T(8,128)(2,1)S(1)}, bf16[64,8,16]{2,0,1:T(8,128)(2,1)S(1)}, u32[]{:S(2)}, u32[]{:S(2)}) collective-permute-start(bf16[64,8,16]{2,0,1:T(8,128)(2,1)S(1)} %fusion.32), channel_id=1, source_target_pairs={{0,1},{1,0},{2,3},{3,2},{4,5},{5,4},{6,7},{7,6},{8,9},{9,8},{10,11... | collective-permute-start | bytes 49160 | tf_op jit(solution)/shard_map/ppermute | solution.py:22
